TPU v7x, 1024 devices: a whole 4x8x16 slice. The times are simulated.
1024 devices in a mesh: blk: 128 (over y, z), rep: 8 (over x, core).
Axes of the slice: x: 4, y: 8, z: 16, core: 2. Of those that a mesh axis runs over, the one named last changes fastest.
Arguments:
- features: bfloat16 [65536, 128], P('blk'), may hold values from -6 to 6
- band_weight: bfloat16 [65536, 16384], P('blk', 'rep'), may hold values from -0.03125 to 0.03125
- far_weight: bfloat16 [65536, 2048], P('blk', 'rep'), may hold values from -0.09375 to 0.09375
- send_rows: int32 [128, 8, 256], P('blk', 'rep'), may hold values from 0 to 511
- layer_one: bfloat16 [128, 256], replicated, may hold values from -0.5 to 0.5
- layer_two: bfloat16 [256, 128], replicated, may hold values from -0.375 to 0.375
- cotangent: bfloat16 [65536, 128], P('blk'), may hold values from -0.0234375 to 0.0234375
Outputs:
- scores: bfloat16 [65536, 128], P('blk')
- weight_grad: float32 [256, 128], replicated
All inputs are finite; a program needn't handle non-finite values.
Results may differ from a plain program's by a relative error of at most 0.0058.
Values may be sent and summed in bfloat16 or wider, within the bound.
A program may use at most 32 MiB of HBM per device.

v0:
```python
import jax
import jax.numpy as jnp
from jax import lax
from jax.sharding import PartitionSpec as P


def shifted_2(value, axis, steps):
    count = lax.axis_size(axis)
    pairs = [(source, (source + steps) % count) for source in range(count)]
    return lax.ppermute(value, axis, pairs)


def move_cycle(value, offset):
    return shifted_2(value, "blk", offset)


def sum_replicas(value):
    return lax.psum(value, "rep")


def unchanged(value):
    return value


def aggregate(node_values, band_block, far_block, send_block, expand):
    row_count = node_values.shape[0]
    step_count = band_block.shape[1] // row_count
    replica = lax.axis_index("rep")
    moving = node_values
    for bit_index in range((lax.axis_size("rep") - 1).bit_length()):
        shifted = move_cycle(moving, step_count << bit_index)
        moving = jnp.where(replica >> bit_index & 1 == 1, shifted, moving)
    summed = None
    for step_index in range(step_count):
        if step_index > 0:
            moving = move_cycle(moving, 1)
        band_slice = band_block[:, step_index * row_count : (step_index + 1) * row_count]
        term = jnp.dot(band_slice, expand(moving), preferred_element_type=jnp.float32)
        summed = term if summed is None else summed + term
    outgoing = jnp.take(node_values, send_block.reshape(-1), axis=0)
    arrived = expand(lax.all_to_all(outgoing, "blk", split_axis=0, concat_axis=0, tiled=True))
    return summed + jnp.dot(far_block, arrived, preferred_element_type=jnp.float32)


def per_device(features, band_weight, far_weight, send_rows, layer_one, layer_two, cotangent):
    layer_input = sum_replicas(
        aggregate(features, band_weight, far_weight, send_rows, unchanged)
    ).astype(jnp.bfloat16)
    second = aggregate(
        jax.nn.relu(jnp.dot(layer_input, layer_one, preferred_element_type=jnp.float32)).astype(
            jnp.bfloat16
        ),
        band_weight,
        far_weight,
        send_rows,
        unchanged,
    )
    project = layer_two.astype(jnp.float32)
    target = cotangent.astype(jnp.float32)
    contract = (((0,), (0,)), ((), ()))
    summed = sum_replicas(second)
    scores = jnp.dot(summed, project, precision=lax.Precision.HIGHEST).astype(jnp.bfloat16)
    share_rows = summed.shape[0] // lax.axis_size("rep")
    row_start = lax.axis_index("rep") * share_rows
    own_rows = lax.dynamic_slice_in_dim(summed, row_start, share_rows, 0)
    own_target = lax.dynamic_slice_in_dim(target, row_start, share_rows, 0)
    grad_term = lax.dot_general(own_rows, own_target, contract, precision=lax.Precision.HIGHEST)
    weight_grad = lax.psum(grad_term, ("blk", "rep"))
    return (scores, weight_grad)


def solution(mesh):
    return jax.shard_map(
        per_device,
        mesh=mesh,
        in_specs=(
            P("blk", None),
            P("blk", "rep"),
            P("blk", "rep"),
            P("blk", "rep", None),
            P(),
            P(),
            P("blk", None),
        ),
        out_specs=(P("blk", None), P()),
        check_vma=False,
    )
```

profile of v0, /device:TPU:1, one launch (start us, length us, event | category | flops | bytes accessed | tf_op | source)
XLA Modules:
  0.0 805.9 jit_solution(14855271661125978812)
XLA Ops:
  7.2 0.0 copy-start
  7.2 0.0 copy-start.1
  7.2 11.6 %collective-permute-start = (bf16[512,128]{1,0:T(8,128)(2,1)}, bf16[512,128]{1,0:T(8,128)(2,1)S(1)}, u32[]{:S(2)}, u32[]{:S(2)}) collective-permute-start(bf16[512,128]{1,0:T(8,128)(2,1)} %param.7), channel_id=1, source_target_pairs={{0,32},{8,40},{16,48},{24,56},{32,64},{40,72},{48,80},{56,88},{64,... | collective-permute-start | bytes 393224 | tf_op jit(solution)/shard_map/ppermute | solution.py:10
  18.8 0.7 compare_select_fusion.1
  19.5 0.5 broadcast.43
  20.0 1.3 reduce.3
  21.3 0.1 reshape.59
  21.5 1.7 gather_fusion
  23.1 8.7 %collective-permute-done = bf16[512,128]{1,0:T(8,128)(2,1)S(1)} collective-permute-done((bf16[512,128]{1,0:T(8,128)(2,1)}, bf16[512,128]{1,0:T(8,128)(2,1)S(1)}, u32[]{:S(2)}, u32[]{:S(2)}) %collective-permute-start) | collective-permute-done | bytes 131104 | tf_op jit(solution)/shard_map/ppermute | solution.py:10
  31.8 13.1 %collective-permute-start.1 = (bf16[512,128]{1,0:T(8,128)(2,1)S(1)}, bf16[512,128]{1,0:T(8,128)(2,1)S(1)}, u32[]{:S(2)}, u32[]{:S(2)}) collective-permute-start(bf16[512,128]{1,0:T(8,128)(2,1)S(1)} %broadcast_select_fusion.5), channel_id=1, source_target_pairs={{0,64},{8,72},{16,80},{24,88},{32,96},{40,104},{48,112},{56,120},{... | collective-permute-start | bytes 393224 | tf_op jit(solution)/shard_map/ppermute | solution.py:10
  45.0 6.7 collective-permute-done.1
  51.7 1.9 collective-permute-start.2
  53.6 0.8 broadcast_select_fusion.4
  54.5 22.5 %all-to-all-start = ((bf16[128,2,128]{2,1,0:T(2,128)(2,1)}), bf16[128,2,128]{2,1,0:T(2,128)(2,1)S(1)}, u32[]{:S(2)}, u32[]{:S(2)}) async-start(bf16[128,2,128]{2,1,0:T(2,128)(2,1)} %broadcast_select_fusion.4), calls=%async_computation | async-start | bytes 131072 | tf_op jit(solution)/shard_map/all_to_all | solution.py:41
  77.0 0.0 collective-permute-done.2
  77.0 2.5 collective-permute-start.3
  79.5 12.4 %all-to-all-done = bf16[128,2,128]{2,1,0:T(2,128)(2,1)S(1)} async-done(((bf16[128,2,128]{2,1,0:T(2,128)(2,1)}), bf16[128,2,128]{2,1,0:T(2,128)(2,1)S(1)}, u32[]{:S(2)}, u32[]{:S(2)}) %all-to-all-start) | async-done | bytes 65568 | tf_op jit(solution)/shard_map/all_to_all | solution.py:41
  92.0 0.2 fusion.20
  92.2 0.0 collective-permute-done.3
  92.2 2.3 collective-permute-start.4
  94.5 0.3 fusion.11
  94.8 0.0 copy-start.2
  94.8 0.3 convolution_add_fusion.5
  95.1 6.1 collective-permute-done.4
  101.2 1.9 collective-permute-start.5
  103.2 0.3 convolution_add_fusion.4
  103.5 6.8 collective-permute-done.5
  110.3 0.3 fusion.4
  110.6 30.0 %all-reduce.7 = bf16[512,128]{0,1:T(8,128)(2,1)S(1)} all-reduce(f32[512,128]{0,1:T(8,128)S(1)} %fusion.4), channel_id=1, replica_groups=mesh['blk'=128,'rep'=8] {'rep'}, use_global_device_ids=true, to_apply=%region_0.1 | all-reduce | flops 65536 | bytes 393216 | tf_op jit(solution)/shard_map/psum | solution.py:18
  140.6 0.2 fusion.2
  140.9 1.9 collective-permute-start.6
  142.8 25.2 %collective-permute-done.6 = bf16[512,256]{1,0:T(8,128)(2,1)S(1)} collective-permute-done((bf16[512,256]{1,0:T(8,128)(2,1)S(1)}, bf16[512,256]{1,0:T(8,128)(2,1)S(1)}, u32[]{:S(2)}, u32[]{:S(2)}) %collective-permute-start.6) | collective-permute-done | bytes 262176 | tf_op jit(solution)/shard_map/ppermute | solution.py:10
  168.0 2.6 collective-permute-start.7
  170.6 1.2 gather_fusion.1
  171.8 0.1 gather.15
  171.8 17.4 %collective-permute-done.7 = bf16[512,256]{1,0:T(8,128)(2,1)S(1)} collective-permute-done((bf16[512,256]{1,0:T(8,128)(2,1)S(1)}, bf16[512,256]{1,0:T(8,128)(2,1)S(1)}, u32[]{:S(2)}, u32[]{:S(2)}) %collective-permute-start.7) | collective-permute-done | bytes 262176 | tf_op jit(solution)/shard_map/ppermute | solution.py:10
  189.3 4.6 collective-permute-start.8
  193.9 0.9 broadcast_select_fusion
  194.8 12.6 %all-to-all-start.1 = ((bf16[128,2,256]{2,1,0:T(2,128)(2,1)}), bf16[128,2,256]{2,1,0:T(2,128)(2,1)S(1)}, u32[]{:S(2)}, u32[]{:S(2)}) async-start(bf16[128,2,256]{2,1,0:T(2,128)(2,1)} %broadcast_select_fusion), calls=%async_computation.1 | async-start | bytes 262144 | tf_op jit(solution)/shard_map/all_to_all | solution.py:41
  207.4 0.0 all-reduce.4.cloned.1.call-start
  207.4 0.0 collective-permute-done.8
  207.5 2.5 collective-permute-start.9
  210.0 13.6 %all-to-all-done.1 = bf16[128,2,256]{2,1,0:T(2,128)(2,1)S(1)} async-done(((bf16[128,2,256]{2,1,0:T(2,128)(2,1)}), bf16[128,2,256]{2,1,0:T(2,128)(2,1)S(1)}, u32[]{:S(2)}, u32[]{:S(2)}) %all-to-all-start.1) | async-done | bytes 131104 | tf_op jit(solution)/shard_map/all_to_all | solution.py:41
  223.6 0.1 all_to_all.15
  223.6 0.3 fusion.21
  223.9 0.0 collective-permute-done.9
  223.9 0.3 fusion.9
  224.3 2.4 collective-permute-start.10
  226.6 0.4 convolution_add_fusion.2
  227.0 7.7 collective-permute-done.10
  234.7 1.9 collective-permute-start.11
  236.6 0.4 convolution_add_fusion.1
  237.0 0.0 copy-start.3
  237.0 8.1 %collective-permute-done.11 = bf16[512,256]{1,0:T(8,128)(2,1)S(1)} collective-permute-done((bf16[512,256]{1,0:T(8,128)(2,1)S(1)}, bf16[512,256]{1,0:T(8,128)(2,1)S(1)}, u32[]{:S(2)}, u32[]{:S(2)}) %collective-permute-start.11) | collective-permute-done | bytes 262176 | tf_op jit(solution)/shard_map/ppermute | solution.py:10
  245.1 1.2 fusion.1
  246.3 0.0 all-reduce.4.cloned.1.call-update
  246.3 0.0 all-reduce.6.cloned.1.call-start
  246.4 79.3 %all-reduce.4.cloned.1.call-done = f32[512,256]{0,1:T(8,128)} async-done(((f32[512,256]{0,1:T(8,128)}), f32[512,256]{0,1:T(8,128)}) %all-reduce.4.cloned.1.call-update) | async-done | bytes 524304 | tf_op jit(solution)/shard_map/psum | solution.py:18
  325.7 1.8 fusion.15
  327.5 0.0 all-reduce.6.cloned.1.call-update
  327.5 0.0 copy-done.3
  327.5 2.3 convolution_convert_fusion
  329.8 467.6 %all-reduce.6.cloned.1.call-done = f32[256,128]{1,0:T(8,128)} async-done(((f32[256,128]{1,0:T(8,128)}), f32[256,128]{1,0:T(8,128)}) %all-reduce.6.cloned.1.call-update) | async-done | bytes 131088 | tf_op jit(solution)/shard_map/psum | solution.py:68
  797.5 1.6 copy.13
  (11 shorter events, 0.2 us)
Async XLA Ops:
  7.2 84.8 %copy-start = (bf16[512,256]{1,0:T(8,128)(2,1)S(1)}, bf16[512,256]{1,0:T(8,128)(2,1)}, u32[]{:S(2)}) copy-start(bf16[512,256]{1,0:T(8,128)(2,1)} %param.9) | copy-start | bytes 786436
  7.2 87.3 %copy-start.1 = (bf16[512,2048]{1,0:T(8,128)(2,1)S(1)}, bf16[512,2048]{1,0:T(8,128)(2,1)}, u32[]{:S(2)}) copy-start(bf16[512,2048]{1,0:T(8,128)(2,1)} %param.8) | copy-start | bytes 6291460
  7.2 24.6 %collective-permute-start = (bf16[512,128]{1,0:T(8,128)(2,1)}, bf16[512,128]{1,0:T(8,128)(2,1)S(1)}, u32[]{:S(2)}, u32[]{:S(2)}) collective-permute-start(bf16[512,128]{1,0:T(8,128)(2,1)} %param.7), channel_id=1, source_target_pairs={{0,32},{8,40},{16,48},{24,56},{32,64},{40,72},{48,80},{56,88},{64,... | collective-permute-start | bytes 393224 | tf_op jit(solution)/shard_map/ppermute | solution.py:10
  31.8 19.8 %collective-permute-start.1 = (bf16[512,128]{1,0:T(8,128)(2,1)S(1)}, bf16[512,128]{1,0:T(8,128)(2,1)S(1)}, u32[]{:S(2)}, u32[]{:S(2)}) collective-permute-start(bf16[512,128]{1,0:T(8,128)(2,1)S(1)} %broadcast_select_fusion.5), channel_id=1, source_target_pairs={{0,64},{8,72},{16,80},{24,88},{32,96},{40,104},{48,112},{56,120},{... | collective-permute-start | bytes 393224 | tf_op jit(solution)/shard_map/ppermute | solution.py:10
  51.7 25.3 %collective-permute-start.2 = (bf16[512,128]{1,0:T(8,128)(2,1)S(1)}, bf16[512,128]{1,0:T(8,128)(2,1)S(1)}, u32[]{:S(2)}, u32[]{:S(2)}) collective-permute-start(bf16[512,128]{1,0:T(8,128)(2,1)S(1)} %broadcast_select_fusion.6), channel_id=1, source_target_pairs={{0,128},{8,136},{16,144},{24,152},{32,160},{40,168},{48,176},{56,1... | collective-permute-start | bytes 393224 | tf_op jit(solution)/shard_map/ppermute | solution.py:10
  54.5 37.5 %all-to-all-start = ((bf16[128,2,128]{2,1,0:T(2,128)(2,1)}), bf16[128,2,128]{2,1,0:T(2,128)(2,1)S(1)}, u32[]{:S(2)}, u32[]{:S(2)}) async-start(bf16[128,2,128]{2,1,0:T(2,128)(2,1)} %broadcast_select_fusion.4), calls=%async_computation | async-start | bytes 131072 | tf_op jit(solution)/shard_map/all_to_all | solution.py:41
  77.0 15.2 %collective-permute-start.3 = (bf16[512,128]{1,0:T(8,128)(2,1)S(1)}, bf16[512,128]{1,0:T(8,128)(2,1)S(1)}, u32[]{:S(2)}, u32[]{:S(2)}) collective-permute-start(bf16[512,128]{1,0:T(8,128)(2,1)S(1)} %broadcast_select_fusion.7), channel_id=1, source_target_pairs={{0,8},{8,16},{16,24},{24,32},{32,40},{40,48},{48,56},{56,64},{64,7... | collective-permute-start | bytes 393224 | tf_op jit(solution)/shard_map/ppermute | solution.py:10
  92.2 9.0 %collective-permute-start.4 = (bf16[512,128]{1,0:T(8,128)(2,1)S(1)}, bf16[512,128]{1,0:T(8,128)(2,1)S(1)}, u32[]{:S(2)}, u32[]{:S(2)}) collective-permute-start(bf16[512,128]{1,0:T(8,128)(2,1)S(1)} %collective-permute-done.3), channel_id=1, source_target_pairs={{0,8},{8,16},{16,24},{24,32},{32,40},{40,48},{48,56},{56,64},{64,7... | collective-permute-start | bytes 393224 | tf_op jit(solution)/shard_map/ppermute | solution.py:10
  94.8 45.8 %copy-start.2 = (bf16[128,256]{1,0:T(8,128)(2,1)S(1)}, bf16[128,256]{1,0:T(8,128)(2,1)}, u32[]{:S(2)}) copy-start(bf16[128,256]{1,0:T(8,128)(2,1)} %param.11) | copy-start | bytes 196612
  101.2 9.0 %collective-permute-start.5 = (bf16[512,128]{1,0:T(8,128)(2,1)S(1)}, bf16[512,128]{1,0:T(8,128)(2,1)S(1)}, u32[]{:S(2)}, u32[]{:S(2)}) collective-permute-start(bf16[512,128]{1,0:T(8,128)(2,1)S(1)} %collective-permute-done.4), channel_id=1, source_target_pairs={{0,8},{8,16},{16,24},{24,32},{32,40},{40,48},{48,56},{56,64},{64,7... | collective-permute-start | bytes 393224 | tf_op jit(solution)/shard_map/ppermute | solution.py:10
  140.9 27.1 %collective-permute-start.6 = (bf16[512,256]{1,0:T(8,128)(2,1)S(1)}, bf16[512,256]{1,0:T(8,128)(2,1)S(1)}, u32[]{:S(2)}, u32[]{:S(2)}) collective-permute-start(bf16[512,256]{1,0:T(8,128)(2,1)S(1)} %fusion.2), channel_id=1, source_target_pairs={{0,32},{8,40},{16,48},{24,56},{32,64},{40,72},{48,80},{56,88},{64,... | collective-permute-start | bytes 786440 | tf_op jit(solution)/shard_map/ppermute | solution.py:10
  168.0 21.2 %collective-permute-start.7 = (bf16[512,256]{1,0:T(8,128)(2,1)S(1)}, bf16[512,256]{1,0:T(8,128)(2,1)S(1)}, u32[]{:S(2)}, u32[]{:S(2)}) collective-permute-start(bf16[512,256]{1,0:T(8,128)(2,1)S(1)} %broadcast_select_fusion.1), channel_id=1, source_target_pairs={{0,64},{8,72},{16,80},{24,88},{32,96},{40,104},{48,112},{56,120},{... | collective-permute-start | bytes 786440 | tf_op jit(solution)/shard_map/ppermute | solution.py:10
  189.3 18.2 %collective-permute-start.8 = (bf16[512,256]{1,0:T(8,128)(2,1)S(1)}, bf16[512,256]{1,0:T(8,128)(2,1)S(1)}, u32[]{:S(2)}, u32[]{:S(2)}) collective-permute-start(bf16[512,256]{1,0:T(8,128)(2,1)S(1)} %broadcast_select_fusion.2), channel_id=1, source_target_pairs={{0,128},{8,136},{16,144},{24,152},{32,160},{40,168},{48,176},{56,1... | collective-permute-start | bytes 786440 | tf_op jit(solution)/shard_map/ppermute | solution.py:10
  194.8 28.8 %all-to-all-start.1 = ((bf16[128,2,256]{2,1,0:T(2,128)(2,1)}), bf16[128,2,256]{2,1,0:T(2,128)(2,1)S(1)}, u32[]{:S(2)}, u32[]{:S(2)}) async-start(bf16[128,2,256]{2,1,0:T(2,128)(2,1)} %broadcast_select_fusion), calls=%async_computation.1 | async-start | bytes 262144 | tf_op jit(solution)/shard_map/all_to_all | solution.py:41
  207.4 118.3 %all-reduce.4.cloned.1.call-start = ((), (), s32[]{:S(2)}) async-start(), calls=%async_computation.2 | async-start | bytes 1048576 | tf_op jit(solution)/shard_map/psum | solution.py:18
  207.5 16.4 %collective-permute-start.9 = (bf16[512,256]{1,0:T(8,128)(2,1)S(1)}, bf16[512,256]{1,0:T(8,128)(2,1)S(1)}, u32[]{:S(2)}, u32[]{:S(2)}) collective-permute-start(bf16[512,256]{1,0:T(8,128)(2,1)S(1)} %broadcast_select_fusion.3), channel_id=1, source_target_pairs={{0,8},{8,16},{16,24},{24,32},{32,40},{40,48},{48,56},{56,64},{64,7... | collective-permute-start | bytes 786440 | tf_op jit(solution)/shard_map/ppermute | solution.py:10
  224.3 10.4 %collective-permute-start.10 = (bf16[512,256]{1,0:T(8,128)(2,1)S(1)}, bf16[512,256]{1,0:T(8,128)(2,1)S(1)}, u32[]{:S(2)}, u32[]{:S(2)}) collective-permute-start(bf16[512,256]{1,0:T(8,128)(2,1)S(1)} %collective-permute-done.9), channel_id=1, source_target_pairs={{0,8},{8,16},{16,24},{24,32},{32,40},{40,48},{48,56},{56,64},{64,7... | collective-permute-start | bytes 786440 | tf_op jit(solution)/shard_map/ppermute | solution.py:10
  234.7 10.4 %collective-permute-start.11 = (bf16[512,256]{1,0:T(8,128)(2,1)S(1)}, bf16[512,256]{1,0:T(8,128)(2,1)S(1)}, u32[]{:S(2)}, u32[]{:S(2)}) collective-permute-start(bf16[512,256]{1,0:T(8,128)(2,1)S(1)} %collective-permute-done.10), channel_id=1, source_target_pairs={{0,8},{8,16},{16,24},{24,32},{32,40},{40,48},{48,56},{56,64},{64,7... | collective-permute-start | bytes 786440 | tf_op jit(solution)/shard_map/ppermute | solution.py:10
  237.0 90.5 %copy-start.3 = (bf16[256,128]{1,0:T(8,128)(2,1)S(1)}, bf16[256,128]{1,0:T(8,128)(2,1)}, u32[]{:S(2)}) copy-start(bf16[256,128]{1,0:T(8,128)(2,1)} %param.12) | copy-start | bytes 196612
  246.3 551.2 %all-reduce.6.cloned.1.call-start = ((), (), s32[]{:S(2)}) async-start(), calls=%async_computation.3 | async-start | bytes 262144 | tf_op jit(solution)/shard_map/psum | solution.py:68
Sparse Core Ops, SparseCore 0:
  246.4 79.2 all-reduce.3
  332.6 464.8 all-reduce.5
where the time goes:
time: 807 us; the launch traced here: 806 us
  waiting for transfers between devices  660 us (82%)
  starting transfers between devices  84.3 us (10%)
  blocking collectives  30 us (4%)
  between operations  14.4 us (2%)
  matrix products  8.31 us (1%)
    psum x1, waiting for transfers between devices, per_device(): weight_grad = lax.psum(grad_term, ('blk', 'rep'))  468 us
    ppermute x12, waiting for transfers between devices, shifted_2(): return lax.ppermute(value, axis, pairs)  86.7 us
    psum x1, waiting for transfers between devices, sum_replicas(): return lax.psum(value, 'rep')  79.3 us
    ppermute x12, starting transfers between devices, shifted_2(): return lax.ppermute(value, axis, pairs)  49.2 us
    all_to_all x2, starting transfers between devices, aggregate(): lax.all_to_all(outgoing, 'blk', split_axis=0, concat_axis=0, tiled=True)  35.1 us
    psum x1, blocking collectives, sum_replicas(): return lax.psum(value, 'rep')  30 us
    all_to_all x2, waiting for transfers between devices, aggregate(): lax.all_to_all(outgoing, 'blk', split_axis=0, concat_axis=0, tiled=True)  26 us
  transfers between devices with their start and end apart: 16, of which 12 were waited for; matrix products, arithmetic and copies ran while one was open for 1% of the time, Pallas kernels for 0%

commit v1 on v0

v1 whole, which is shorter than its diff:
```python
import functools

import jax
import jax.numpy as jnp
from jax import lax
from jax.experimental import pallas as pl
from jax.experimental.pallas import tpu as pltpu
from jax.sharding import PartitionSpec as P

MESH = pl.DeviceIdType.MESH
BF16 = jnp.bfloat16
F32 = jnp.float32

Y, Z, R = 8, 16, 8
N = Y * Z
ROWS = 512
FEAT = 128
HID = 256
STEPS = 4
PIECE = ROWS // R
SLOTS = 2 * N
GROUPS = Y * R
SHARE = HID // GROUPS


def dot(a, b):
    return jnp.dot(a, b, preferred_element_type=F32)


def dot_rows(a, b):
    return lax.dot_general(a, b, (((0,), (0,)), ((), ())), preferred_element_type=F32)


def split(value):
    high = value.astype(BF16)
    return high, (value - high.astype(F32)).astype(BF16)


def kernel(
    feat_hbm, band_hbm, far_hbm, rows_ref, one_hbm, two_hbm, cot_hbm,
    scores_ref, grad_ref,
    feat, band, far, one, two, cot, pick, total,
    send_far, recv_far, relay, blocks, whole, cut, shares,
    grad_cut, grad_in, grad_z, grad_out, score_cut, score_in, score_own, score_all,
    load_sem, y_sem, rep_sem,
    far_send, far_recv, own_far, relay_send, relay_recv, block_send, block_recv,
    cut_send, cut_recv, whole_send, whole_recv,
    grad_send, grad_recv, z_send, z_recv, out_send, out_recv,
    sc_send, sc_recv, sa_send, sa_recv,
):
    i, r = lax.axis_index("blk"), lax.axis_index("rep")
    y, z = i // Z, lax.rem(i, Z)
    own = pl.ds(pl.multiple_of(r * PIECE, PIECE), PIECE)

    def at(index):
        return lax.rem(index + N, N)

    def remote(src, dst, send, recv, blk, rep):
        return pltpu.make_async_remote_copy(
            src_ref=src, dst_ref=dst, send_sem=send, recv_sem=recv, device_id=(blk, rep), device_id_type=MESH
        )

    def wait_in(ref, recv):
        remote(ref, ref, recv, recv, i, r).wait_recv()

    def wait_out(ref, send):
        remote(ref, ref, send, send, i, r).wait_send()

    def z_peer(d):
        return y * Z + lax.rem(z + d, Z)

    def y_peer(d):
        return lax.rem(i + d * Z, N)

    def rep_peer(d):
        return lax.rem(r + d, R)

    barrier = pltpu.get_barrier_semaphore()
    for d in range(1, Z):
        pl.semaphore_signal(barrier, inc=1, device_id=(z_peer(d), r), device_id_type=MESH)
    for d in range(1, Y):
        pl.semaphore_signal(barrier, inc=1, device_id=(y_peer(d), r), device_id_type=MESH)
    for d in range(1, R):
        pl.semaphore_signal(barrier, inc=1, device_id=(i, rep_peer(d)), device_id_type=MESH)

    loads = [
        pltpu.make_async_copy(src, dst, load_sem.at[n])
        for n, (src, dst) in enumerate(
            [(feat_hbm, feat), (band_hbm, band), (far_hbm, far), (one_hbm, one), (two_hbm, two), (cot_hbm, cot)]
        )
    ]
    for load in loads:
        load.start()
    spot = lax.broadcasted_iota(jnp.int32, (ROWS, SLOTS), 0)
    pick[...] = jnp.where(spot == rows_ref[...], 1.0, 0.0).astype(BF16)
    loads[0].wait()

    def gather(layer, source):
        rows = dot_rows(pick[...], source[...]).astype(BF16)
        send_far[layer] = rows.reshape(N, 2, FEAT)

    gather(0, feat)
    pl.semaphore_wait(barrier, Z + Y + R - 3)
    for d in range(1, Y):
        pl.semaphore_signal(y_sem, inc=1, device_id=(y_peer(d), r), device_id_type=MESH)
    pl.semaphore_wait(y_sem, Y - 1)
    for d in range(1, R):
        pl.semaphore_signal(rep_sem, inc=1, device_id=(i, rep_peer(d)), device_id_type=MESH)

    def far_start(layer):
        @pl.loop(1, N)
        def _(d):
            to = at(i + d)
            remote(
                send_far.at[layer, to], recv_far.at[layer, i], far_send.at[layer], far_recv.at[layer], to, r
            ).start()

        pltpu.make_async_copy(send_far.at[layer, i], recv_far.at[layer, i], own_far.at[layer]).start()

    def far_wait(layer):
        wait_in(recv_far.at[layer, pl.ds(0, N - 1)], far_recv.at[layer])
        pltpu.make_async_copy(send_far.at[layer, i], recv_far.at[layer, i], own_far.at[layer]).wait()
        return recv_far[layer].reshape(SLOTS, FEAT)

    def relay_start(layer, piece):
        for rep in range(1, R):
            down = rep % 4 // 2
            remote(
                piece, relay.at[layer, rep], relay_send.at[layer], relay_recv.at[layer, rep],
                at(i + 4 * rep + 3 * down), r,
            ).start()

    def relay_on(layer, piece):
        for step in range(1, STEPS):
            remote(
                piece, blocks.at[layer, step, own], block_send.at[layer], block_recv.at[layer, step], at(i + step), 0
            ).start()
        for rep in (1, 5, 2, 6, 3, 7, 4):
            down = rep % 4 // 2
            wait_in(relay.at[layer, rep], relay_recv.at[layer, rep])
            for k in range(STEPS):
                step = STEPS - 1 - k if down else k
                src, dst = relay.at[layer, rep], blocks.at[layer, step, own]
                copy = remote(
                    src, dst, block_send.at[layer], block_recv.at[layer, step], at(i - k if down else i + k), rep
                )
                if k:
                    copy.start()
                else:
                    pl.when(r != rep)(copy.start)

                    @pl.when(r == rep)
                    def _():
                        pltpu.make_async_copy(src, dst, block_recv.at[layer, step]).start()

    def own_block(layer, source):
        @pl.when(r == 0)
        def _():
            pltpu.make_async_copy(source, blocks.at[layer, 0], block_recv.at[layer, 0]).start()

    far_start(0)
    relay_start(0, feat.at[own])
    own_block(0, feat)
    pl.semaphore_wait(rep_sem, R - 1)
    relay_on(0, feat.at[own])
    for load in loads[1:]:
        load.wait()
    for step in range(STEPS):
        wait_in(blocks.at[0, step], block_recv.at[0, step])
        term = dot(band[:, step * ROWS : (step + 1) * ROWS], blocks[0, step])
        total[:, :FEAT] = term if step == 0 else total[:, :FEAT] + term
    total[:, :FEAT] += dot(far[...], far_wait(0))

    def cut_start(source, cut_ref, in_ref, send, recv):
        cut_ref[...] = source.reshape(R, PIECE, FEAT).astype(BF16)
        for d in range(1, R):
            to = rep_peer(d)
            remote(cut_ref.at[to], in_ref.at[r], send, recv, i, to).start()

    def cut_sum(own_rows, in_ref, recv):
        in_ref[r] = jnp.zeros((PIECE, FEAT), BF16)
        wait_in(in_ref.at[pl.ds(0, R - 1)], recv)
        return own_rows + jnp.sum(in_ref[...].astype(F32), axis=0)

    cut_start(total[:, :FEAT], cut, shares, cut_send, cut_recv)
    whole[own] = cut_sum(total[own, :FEAT], shares, cut_recv).astype(BF16)
    for d in range(1, R):
        remote(whole.at[own], whole.at[own], whole_send, whole_recv, i, rep_peer(d)).start()
    relay_start(1, whole.at[own])
    wait_in(whole.at[pl.ds(0, ROWS - PIECE)], whole_recv)
    gather(1, whole)
    far_start(1)
    own_block(1, whole)
    relay_on(1, whole.at[own])

    def expand(value):
        return jnp.maximum(dot(value, one[...]), 0.0).astype(BF16)

    for step in range(STEPS):
        wait_in(blocks.at[1, step], block_recv.at[1, step])
        term = dot(band[:, step * ROWS : (step + 1) * ROWS], expand(blocks[1, step]))
        total[...] = term if step == 0 else total[...] + term
    total[...] += dot(far[...], expand(far_wait(1)))
    high, low = split(total[...])

    local = dot_rows(high, cot[...]) + dot_rows(low, cot[...])
    grad_cut[...] = local.reshape(GROUPS, SHARE, FEAT).astype(BF16)
    mine = y * R + r

    def group_loop(body):
        @pl.loop(1, GROUPS)
        def _(d):
            to_y, to_r = lax.rem(y + d // R, Y), lax.rem(r + lax.rem(d, R), R)
            body(to_y * R + to_r, to_y * Z + z, to_r)

    def grad_go(slot, blk, rep):
        remote(grad_cut.at[slot], grad_in.at[mine], grad_send, grad_recv, blk, rep).start()

    group_loop(grad_go)

    part = dot(high, two[...]) + dot(low, two[...])
    score_own[...] = part.reshape(R, PIECE, FEAT)
    cut_start(part, score_cut, score_in, sc_send, sc_recv)

    grad_in[mine] = grad_cut[mine]
    wait_in(grad_in.at[pl.ds(0, GROUPS - 1)], grad_recv)
    grad_z[z] = jnp.sum(grad_in[...].astype(F32), axis=0)
    for d in range(1, Z):
        remote(grad_z.at[z], grad_z.at[z], z_send, z_recv, z_peer(d), r).start()

    score_all[own] = cut_sum(score_own[r], score_in, sc_recv).astype(BF16)
    for d in range(1, R):
        remote(score_all.at[own], score_all.at[own], sa_send, sa_recv, i, rep_peer(d)).start()

    wait_in(grad_z.at[pl.ds(0, Z - 1)], z_recv)
    grad_out[mine] = jnp.sum(grad_z[...], axis=0).astype(BF16)

    def out_go(slot, blk, rep):
        remote(grad_out.at[mine], grad_out.at[mine], out_send, out_recv, blk, rep).start()

    group_loop(out_go)
    wait_in(score_all.at[pl.ds(0, ROWS - PIECE)], sa_recv)
    scores_ref[...] = score_all[...]
    wait_in(grad_out.at[pl.ds(0, GROUPS - 1)], out_recv)
    grad_ref[...] = grad_out[...].astype(F32).reshape(HID, FEAT)

    for layer in range(2):
        wait_out(recv_far.at[layer, pl.ds(0, N - 1)], far_send.at[layer])
        wait_out(relay.at[layer, pl.ds(1, R - 1)], relay_send.at[layer])
        wait_out(relay.at[layer, pl.ds(1, 3)], block_send.at[layer])
        for k in range(STEPS - 1):
            wait_out(relay.at[layer, pl.ds(1, R - 1)], block_send.at[layer])
        wait_out(relay.at[layer, pl.ds(1, R - 2)], block_send.at[layer])
        pl.when(r == 0)(lambda: wait_out(relay.at[layer, 1], block_send.at[layer]))
    wait_out(shares.at[pl.ds(0, R - 1)], cut_send)
    wait_out(whole.at[pl.ds(0, ROWS - PIECE)], whole_send)
    wait_out(score_in.at[pl.ds(0, R - 1)], sc_send)
    wait_out(score_all.at[pl.ds(0, ROWS - PIECE)], sa_send)
    wait_out(grad_in.at[pl.ds(0, GROUPS - 1)], grad_send)
    wait_out(grad_z.at[pl.ds(0, Z - 1)], z_send)
    wait_out(grad_out.at[pl.ds(0, GROUPS - 1)], out_send)


def per_device(features, band_weight, far_weight, send_rows, layer_one, layer_two, cotangent):
    dma, regular, vmem = pltpu.SemaphoreType.DMA, pltpu.SemaphoreType.REGULAR, pltpu.VMEM
    anywhere = pl.BlockSpec(memory_space=pl.ANY)
    here = pl.BlockSpec(memory_space=pltpu.VMEM)
    scratch = [
        vmem((ROWS, FEAT), BF16),
        vmem((ROWS, STEPS * ROWS), BF16),
        vmem((ROWS, SLOTS), BF16),
        vmem((FEAT, HID), BF16),
        vmem((HID, FEAT), BF16),
        vmem((ROWS, FEAT), BF16),
        vmem((ROWS, SLOTS), BF16),
        vmem((ROWS, HID), F32),
        vmem((2, N, 2, FEAT), BF16),
        vmem((2, N, 2, FEAT), BF16),
        vmem((2, R, PIECE, FEAT), BF16),
        vmem((2, STEPS, ROWS, FEAT), BF16),
        vmem((ROWS, FEAT), BF16),
        vmem((R, PIECE, FEAT), BF16),
        vmem((R, PIECE, FEAT), BF16),
        vmem((GROUPS, SHARE, FEAT), BF16),
        vmem((GROUPS, SHARE, FEAT), BF16),
        vmem((Z, SHARE, FEAT), F32),
        vmem((GROUPS, SHARE, FEAT), BF16),
        vmem((R, PIECE, FEAT), BF16),
        vmem((R, PIECE, FEAT), BF16),
        vmem((R, PIECE, FEAT), F32),
        vmem((ROWS, FEAT), BF16),
        dma((6,)), regular, regular,
        dma((2,)), dma((2,)), dma((2,)), dma((2,)), dma((2, R)), dma((2,)), dma((2, STEPS)),
        dma, dma, dma, dma,
        dma, dma, dma, dma, dma, dma,
        dma, dma, dma, dma,
    ]
    return pl.pallas_call(
        kernel,
        out_shape=(jax.ShapeDtypeStruct((ROWS, FEAT), BF16), jax.ShapeDtypeStruct((HID, FEAT), F32)),
        in_specs=[anywhere, anywhere, anywhere, here, anywhere, anywhere, anywhere],
        out_specs=(here, here),
        scratch_shapes=scratch,
        name="graph",
        compiler_params=pltpu.CompilerParams(collective_id=0, has_side_effects=True, vmem_limit_bytes=60 << 20),
    )(features, band_weight, far_weight, send_rows.reshape(1, SLOTS), layer_one, layer_two, cotangent)


def solution(mesh):
    return jax.shard_map(
        per_device,
        mesh=mesh,
        in_specs=(
            P("blk", None),
            P("blk", "rep"),
            P("blk", "rep"),
            P("blk", "rep", None),
            P(),
            P(),
            P("blk", None),
        ),
        out_specs=(P("blk", None), P()),
        check_vma=False,
    )
```

time: 807 us -> 101 us (0.13)
  waiting for transfers between devices: 660 us -> 0 us
  Pallas kernels: 0 us -> 96.8 us
  starting transfers between devices: 84.3 us -> 0 us
  blocking collectives: 30 us -> 0 us
  between operations: 14.4 us -> 0.64 us
  matrix products: 8.31 us -> 0 us
    psum x2 -> x0, waiting for transfers between devices: 547 us -> none  [the longest x1 468 us: per_device(): weight_grad = lax.psum(grad_term, ('blk', 'rep'))]
    pallas_call x0 -> x1, Pallas kernels: none -> 96.8 us  [per_device(): pl.pallas_call(kernel, out_shape=(jax.ShapeDtypeStruct((ROWS, FEAT), BF16...]
    ppermute x12 -> x0, waiting for transfers between devices: 86.7 us -> none  [shifted_2(): return lax.ppermute(value, axis, pairs)]
    ppermute x12 -> x0, starting transfers between devices: 49.2 us -> none  [shifted_2(): return lax.ppermute(value, axis, pairs)]
    all_to_all x2 -> x0, starting transfers between devices: 35.1 us -> none  [aggregate(): lax.all_to_all(outgoing, 'blk', split_axis=0, concat_axis=0, tiled=True)]
    psum x1 -> x0, blocking collectives: 30 us -> none  [sum_replicas(): return lax.psum(value, 'rep')]
    all_to_all x2 -> x0, waiting for transfers between devices: 26 us -> none  [aggregate(): lax.all_to_all(outgoing, 'blk', split_axis=0, concat_axis=0, tiled=True)]
    dot_general x13 -> x0, matrix products: 8.31 us -> none  [the longest x8 3.45 us: aggregate(): jnp.dot(band_slice, expand(moving), preferred_element_type=jnp.float32)]
  transfers between devices with their start and end apart: 16 -> 0, of which waited for: 12 -> 0; matrix products, arithmetic and copies ran while one was open for 1% -> 0% of each run, Pallas kernels for 0% -> 0%
where the time goes in v1:
time: 101 us
  Pallas kernels  96.8 us (96%)
  local copies, waits for them, and re-layouts  3.14 us (3%)
    pallas_call x1, Pallas kernels, per_device(): pl.pallas_call(kernel, out_shape=(jax.ShapeDtypeStruct((ROWS, FEAT), BF16...  96.8 us
    unnamed x2, local copies, waits for them, and re-layouts  3.14 us

profile of v1, /device:TPU:1, one launch (start us, length us, event | category | flops | bytes accessed | tf_op | source)
XLA Modules:
  0.0 100.6 jit_solution(10743887813257960790)
XLA Ops:
  0.6 96.8 %graph.1 = (bf16[512,128]{1,0:T(8,128)(2,1)}, f32[256,128]{1,0:T(8,128)}) custom-call(bf16[512,128]{1,0:T(8,128)(2,1)} %feat_hbm.1, bf16[512,2048]{1,0:T(8,128)(2,1)} %band_hbm.1, bf16[512,256]{1,0:T(8,128)(2,1)} %far_hbm.1, s32[1,256]{1,0:T(1,128)} %bitcast.1, bf16[128,256]{1,0:T(8,128)(2,1)} %one_hbm.1, bf16[256,128]{1,0:T(8,128)(2,1)} %two_hbm.1, ...), custom_call_target="tpu_custom_call" | custom-call | tf_op jit(solution)/shard_map/graph/pallas_call | solution.py:298
  97.4 1.6 %copy.11 = bf16[512,128]{1,0:T(8,128)(2,1)} copy(bf16[512,128]{1,0:T(8,128)(2,1)} %get-tuple-element.4) | data formatting | bytes 262144
  99.0 1.6 %copy.12 = f32[256,128]{1,0:T(8,128)} copy(f32[256,128]{1,0:T(8,128)} %get-tuple-element.5) | data formatting | bytes 262144

commit v2 on v1

v2 whole, which is shorter than its diff:
```python
import functools

import jax
import jax.numpy as jnp
from jax import lax
from jax.experimental import pallas as pl
from jax.experimental.pallas import tpu as pltpu
from jax.sharding import PartitionSpec as P

MESH = pl.DeviceIdType.MESH
BF16 = jnp.bfloat16
F32 = jnp.float32

Y, Z, R = 8, 16, 8
N = Y * Z
ROWS = 512
FEAT = 128
HID = 256
STEPS = 4
PIECE = ROWS // R
SLOTS = 2 * N
GROUPS = Y * R
SHARE = HID // GROUPS
CENTRES = (4, 13, 20, 29, 7, 10, 23, 26)
STRAIGHT = (31, 18, 17, 15, 16, 2, 1)


def far_first(n, size):
    half = (n + 1) // 2
    return size // 2 + half * (1 - 2 * (n % 2))


def dot(a, b):
    return jnp.dot(a, b, preferred_element_type=F32)


def dot_rows(a, b):
    return lax.dot_general(a, b, (((0,), (0,)), ((), ())), preferred_element_type=F32)


def split(value):
    high = value.astype(BF16)
    return high, (value - high.astype(F32)).astype(BF16)


def kernel(
    feat_hbm, band_hbm, far_hbm, rows_ref, one_hbm, two_hbm, cot_hbm,
    scores_hbm, grad_hbm,
    feat, band, far, one, two, cot, pick, total, pulled, pulled_far, local, grad_full,
    send_far, recv_far, relay, blocks, whole, cut, shares,
    grad_cut, grad_in, grad_z, grad_out, score_cut, score_in, score_own, score_all,
    load_sem, save_sem, y_sem, rep_sem,
    far_send, far_recv, own_far, relay_send, relay_recv, block_send, block_recv,
    cut_send, cut_recv, whole_send, whole_recv,
    grad_send, grad_recv, z_send, z_recv, out_send, out_recv,
    sc_send, sc_recv, sa_send, sa_recv,
):
    i, r = lax.axis_index("blk"), lax.axis_index("rep")
    y, z = i // Z, lax.rem(i, Z)
    own = pl.ds(pl.multiple_of(r * PIECE, PIECE), PIECE)

    def at(index):
        return lax.rem(index + N, N)

    def remote(src, dst, send, recv, blk, rep):
        return pltpu.make_async_remote_copy(
            src_ref=src, dst_ref=dst, send_sem=send, recv_sem=recv, device_id=(blk, rep), device_id_type=MESH
        )

    def wait_in(ref, recv):
        remote(ref, ref, recv, recv, i, r).wait_recv()

    def wait_out(ref, send):
        remote(ref, ref, send, send, i, r).wait_send()

    def z_peer(d):
        return y * Z + lax.rem(z + d, Z)

    def y_peer(d):
        return lax.rem(i + d * Z, N)

    def rep_peer(d):
        return lax.rem(r + d, R)

    z_order, y_order, rep_order = ([far_first(n, size) for n in range(size - 1)] for size in (Z, Y, R))

    barrier = pltpu.get_barrier_semaphore()
    for d in z_order:
        pl.semaphore_signal(barrier, inc=1, device_id=(z_peer(d), r), device_id_type=MESH)
    for d in y_order:
        pl.semaphore_signal(barrier, inc=1, device_id=(y_peer(d), r), device_id_type=MESH)
    for d in rep_order:
        pl.semaphore_signal(barrier, inc=1, device_id=(i, rep_peer(d)), device_id_type=MESH)

    loads = [
        pltpu.make_async_copy(src, dst, load_sem.at[n])
        for n, (src, dst) in enumerate(
            [(feat_hbm, feat), (band_hbm, band), (far_hbm, far), (one_hbm, one), (two_hbm, two), (cot_hbm, cot)]
        )
    ]
    for load in loads:
        load.start()
    spot = lax.broadcasted_iota(jnp.int32, (ROWS, SLOTS), 0)
    pick[...] = jnp.where(spot == rows_ref[...], 1.0, 0.0).T.astype(BF16)
    loads[0].wait()

    def gather(layer, source):
        rows = dot(pick[...], source[...]).astype(BF16)
        send_far[layer] = rows.reshape(N, 2, FEAT)

    def pair(ref, value):
        ref[:, :FEAT], ref[:, FEAT:] = split(value)

    gather(0, feat)
    pl.semaphore_wait(barrier, Z + Y + R - 3)
    for d in y_order:
        pl.semaphore_signal(y_sem, inc=1, device_id=(y_peer(d), r), device_id_type=MESH)
    pl.semaphore_wait(y_sem, Y - 1)
    for d in rep_order:
        pl.semaphore_signal(rep_sem, inc=1, device_id=(i, rep_peer(d)), device_id_type=MESH)

    def far_start(layer, low, high):
        @pl.loop(low, high)
        def _(n):
            to_y = lax.rem(y + far_first(lax.rem(n, Y), Y), Y)
            to = to_y * Z + lax.rem(z + far_first(n // Y, Z), Z)
            remote(
                send_far.at[layer, to], recv_far.at[layer, i], far_send.at[layer], far_recv.at[layer], to, r
            ).start()

    def far_own(layer):
        pltpu.make_async_copy(send_far.at[layer, i], recv_far.at[layer, i], own_far.at[layer]).start()

    def far_wait(layer):
        wait_in(recv_far.at[layer, pl.ds(0, N - 1)], far_recv.at[layer])
        pltpu.make_async_copy(send_far.at[layer, i], recv_far.at[layer, i], own_far.at[layer]).wait()
        return recv_far[layer].reshape(SLOTS, FEAT)

    def hand(layer, slot, piece, back):
        remote(
            piece, relay.at[layer, slot], relay_send.at[layer], relay_recv.at[layer, slot], at(i + back), r
        ).start()

    def hand_first(layer, piece):
        for slot in (3, 1, 0, 2):
            hand(layer, slot, piece, CENTRES[slot])

    def straight(layer, piece):
        for back in STRAIGHT:
            rep, step = back // STEPS, back % STEPS
            remote(
                piece, blocks.at[layer, step, own], block_send.at[layer], block_recv.at[layer, step], at(i + back), rep
            ).start()

    def pass_on(layer, slot):
        piece = relay.at[layer, slot]
        wait_in(piece, relay_recv.at[layer, slot])
        if slot < 4:
            hand(layer, slot + 4, piece, CENTRES[slot + 4] - CENTRES[slot])
        for delta in (1, -1):
            rep, step = (CENTRES[slot] + delta) // STEPS, (CENTRES[slot] + delta) % STEPS
            remote(
                piece, blocks.at[layer, step, own], block_send.at[layer], block_recv.at[layer, step], at(i + delta), rep
            ).start()
        rep, step = CENTRES[slot] // STEPS, CENTRES[slot] % STEPS
        dst = blocks.at[layer, step, own]
        copy = remote(piece, dst, block_send.at[layer], block_recv.at[layer, step], i, rep)
        pl.when(r != rep)(copy.start)

        @pl.when(r == rep)
        def _():
            pltpu.make_async_copy(piece, dst, block_recv.at[layer, step]).start()

    def own_block(layer, source):
        @pl.when(r == 0)
        def _():
            pltpu.make_async_copy(source, blocks.at[layer, 0], block_recv.at[layer, 0]).start()

    hand_first(0, feat.at[own])
    far_start(0, 0, N // 2)
    pl.semaphore_wait(rep_sem, R - 1)
    straight(0, feat.at[own])
    for slot in (0, 2, 1, 3):
        pass_on(0, slot)
    far_start(0, N // 2, N - 1)
    far_own(0)
    own_block(0, feat)
    for slot in (4, 6, 5, 7):
        pass_on(0, slot)
    for load in loads[1:]:
        load.wait()
    for step in range(STEPS):
        pair(pulled.at[step], dot_rows(band[:, step * ROWS : (step + 1) * ROWS], cot[...]))
    pair(pulled_far, dot_rows(far[...], cot[...]))
    for step in range(STEPS):
        wait_in(blocks.at[0, step], block_recv.at[0, step])
        term = dot(band[:, step * ROWS : (step + 1) * ROWS], blocks[0, step])
        total[:, :FEAT] = term if step == 0 else total[:, :FEAT] + term
    total[:, :FEAT] += dot(far[...], far_wait(0))

    def cut_start(source, cut_ref, in_ref, send, recv):
        cut_ref[...] = source.reshape(R, PIECE, FEAT).astype(BF16)
        for d in rep_order:
            to = rep_peer(d)
            remote(cut_ref.at[to], in_ref.at[r], send, recv, i, to).start()

    def cut_sum(own_rows, in_ref, recv):
        in_ref[r] = jnp.zeros((PIECE, FEAT), BF16)
        wait_in(in_ref.at[pl.ds(0, R - 1)], recv)
        return own_rows + jnp.sum(in_ref[...].astype(F32), axis=0)

    cut_start(total[:, :FEAT], cut, shares, cut_send, cut_recv)
    whole[own] = cut_sum(total[own, :FEAT], shares, cut_recv).astype(BF16)
    for d in rep_order:
        remote(whole.at[own], whole.at[own], whole_send, whole_recv, i, rep_peer(d)).start()
    hand_first(1, whole.at[own])
    straight(1, whole.at[own])
    wait_in(whole.at[pl.ds(0, ROWS - PIECE)], whole_recv)
    gather(1, whole)
    far_start(1, 0, N // 2)
    for slot in (0, 2, 1, 3):
        pass_on(1, slot)
    far_start(1, N // 2, N - 1)
    far_own(1)
    own_block(1, whole)
    for slot in (4, 6, 5, 7):
        pass_on(1, slot)

    def expand(value):
        return jnp.maximum(dot(value, one[...]), 0.0).astype(BF16)

    for step in range(STEPS):
        wait_in(blocks.at[1, step], block_recv.at[1, step])
        nodes = expand(blocks[1, step])
        term = dot(band[:, step * ROWS : (step + 1) * ROWS], nodes)
        total[...] = term if step == 0 else total[...] + term
        term = dot_rows(nodes, pulled[step])
        local[...] = term if step == 0 else local[...] + term

    far_nodes = expand(far_wait(1))
    term = local[...] + dot_rows(far_nodes, pulled_far[...])
    grad_cut[...] = (term[:, :FEAT] + term[:, FEAT:]).reshape(GROUPS, SHARE, FEAT).astype(BF16)
    mine = y * R + r

    def group_loop(body):
        @pl.loop(0, GROUPS - 1)
        def _(n):
            to_y, to_r = lax.rem(y + far_first(n // R, Y), Y), lax.rem(r + far_first(lax.rem(n, R), R), R)
            body(to_y * R + to_r, to_y * Z + z, to_r)

    def grad_go(slot, blk, rep):
        remote(grad_cut.at[slot], grad_in.at[mine], grad_send, grad_recv, blk, rep).start()

    group_loop(grad_go)

    total[...] += dot(far[...], far_nodes)
    high, low = split(total[...])
    part = dot(high, two[...]) + dot(low, two[...])
    score_own[...] = part.reshape(R, PIECE, FEAT)
    cut_start(part, score_cut, score_in, sc_send, sc_recv)

    grad_in[mine] = grad_cut[mine]
    wait_in(grad_in.at[pl.ds(0, GROUPS - 1)], grad_recv)
    grad_z[z] = jnp.sum(grad_in[...].astype(F32), axis=0)
    for d in z_order:
        remote(grad_z.at[z], grad_z.at[z], z_send, z_recv, z_peer(d), r).start()

    score_all[own] = cut_sum(score_own[r], score_in, sc_recv).astype(BF16)
    for d in rep_order:
        remote(score_all.at[own], score_all.at[own], sa_send, sa_recv, i, rep_peer(d)).start()

    wait_in(grad_z.at[pl.ds(0, Z - 1)], z_recv)
    grad_out[mine] = jnp.sum(grad_z[...], axis=0).astype(BF16)

    def out_go(slot, blk, rep):
        remote(grad_out.at[mine], grad_out.at[mine], out_send, out_recv, blk, rep).start()

    group_loop(out_go)
    wait_in(score_all.at[pl.ds(0, ROWS - PIECE)], sa_recv)
    save_scores = pltpu.make_async_copy(score_all, scores_hbm, save_sem.at[0])
    save_scores.start()
    wait_in(grad_out.at[pl.ds(0, GROUPS - 1)], out_recv)
    grad_full[...] = grad_out[...].astype(F32).reshape(HID, FEAT)
    save_grad = pltpu.make_async_copy(grad_full, grad_hbm, save_sem.at[1])
    save_grad.start()

    for layer in range(2):
        wait_out(recv_far.at[layer, pl.ds(0, N - 1)], far_send.at[layer])
        wait_out(relay.at[layer], relay_send.at[layer])
        wait_out(blocks.at[layer, pl.ds(0, 3)], block_send.at[layer])
        wait_out(relay.at[layer, pl.ds(0, 5)], block_send.at[layer])
        twice = jnp.logical_or(r == 1, r == 5)
        never = jnp.logical_or(r == 0, r == 4)
        pl.when(jnp.logical_not(twice))(lambda: wait_out(relay.at[layer, 0], block_send.at[layer]))
        pl.when(never)(lambda: wait_out(relay.at[layer, 0], block_send.at[layer]))
    wait_out(shares.at[pl.ds(0, R - 1)], cut_send)
    wait_out(whole.at[pl.ds(0, ROWS - PIECE)], whole_send)
    wait_out(score_in.at[pl.ds(0, R - 1)], sc_send)
    wait_out(score_all.at[pl.ds(0, ROWS - PIECE)], sa_send)
    wait_out(grad_in.at[pl.ds(0, GROUPS - 1)], grad_send)
    wait_out(grad_z.at[pl.ds(0, Z - 1)], z_send)
    wait_out(grad_out.at[pl.ds(0, GROUPS - 1)], out_send)
    save_scores.wait()
    save_grad.wait()


def per_device(features, band_weight, far_weight, send_rows, layer_one, layer_two, cotangent):
    dma, regular, vmem = pltpu.SemaphoreType.DMA, pltpu.SemaphoreType.REGULAR, pltpu.VMEM
    anywhere = pl.BlockSpec(memory_space=pl.ANY)
    here = pl.BlockSpec(memory_space=pltpu.VMEM)
    scratch = [
        vmem((ROWS, FEAT), BF16),
        vmem((ROWS, STEPS * ROWS), BF16),
        vmem((ROWS, SLOTS), BF16),
        vmem((FEAT, HID), BF16),
        vmem((HID, FEAT), BF16),
        vmem((ROWS, FEAT), BF16),
        vmem((SLOTS, ROWS), BF16),
        vmem((ROWS, HID), F32),
        vmem((STEPS, ROWS, 2 * FEAT), BF16),
        vmem((SLOTS, 2 * FEAT), BF16),
        vmem((HID, 2 * FEAT), F32),
        vmem((HID, FEAT), F32),
        vmem((2, N, 2, FEAT), BF16),
        vmem((2, N, 2, FEAT), BF16),
        vmem((2, R, PIECE, FEAT), BF16),
        vmem((2, STEPS, ROWS, FEAT), BF16),
        vmem((ROWS, FEAT), BF16),
        vmem((R, PIECE, FEAT), BF16),
        vmem((R, PIECE, FEAT), BF16),
        vmem((GROUPS, SHARE, FEAT), BF16),
        vmem((GROUPS, SHARE, FEAT), BF16),
        vmem((Z, SHARE, FEAT), F32),
        vmem((GROUPS, SHARE, FEAT), BF16),
        vmem((R, PIECE, FEAT), BF16),
        vmem((R, PIECE, FEAT), BF16),
        vmem((R, PIECE, FEAT), F32),
        vmem((ROWS, FEAT), BF16),
        dma((6,)), dma((2,)), regular, regular,
        dma((2,)), dma((2,)), dma((2,)), dma((2,)), dma((2, R)), dma((2,)), dma((2, STEPS)),
        dma, dma, dma, dma,
        dma, dma, dma, dma, dma, dma,
        dma, dma, dma, dma,
    ]
    return pl.pallas_call(
        kernel,
        out_shape=(jax.ShapeDtypeStruct((ROWS, FEAT), BF16), jax.ShapeDtypeStruct((HID, FEAT), F32)),
        in_specs=[anywhere, anywhere, anywhere, here, anywhere, anywhere, anywhere],
        out_specs=(anywhere, anywhere),
        scratch_shapes=scratch,
        name="graph",
        compiler_params=pltpu.CompilerParams(collective_id=0, has_side_effects=True, vmem_limit_bytes=60 << 20),
    )(features, band_weight, far_weight, send_rows.reshape(1, SLOTS), layer_one, layer_two, cotangent)


def solution(mesh):
    return jax.shard_map(
        per_device,
        mesh=mesh,
        in_specs=(
            P("blk", None),
            P("blk", "rep"),
            P("blk", "rep"),
            P("blk", "rep", None),
            P(),
            P(),
            P("blk", None),
        ),
        out_specs=(P("blk", None), P()),
        check_vma=False,
    )
```

time: 101 us -> 95.2 us (0.943)
  Pallas kernels: 96.8 us -> 91.2 us
    pallas_call x1, Pallas kernels: 96.8 us -> 91.2 us  [per_device(): pl.pallas_call(kernel, out_shape=(jax.ShapeDtypeStruct((ROWS, FEAT), BF16...]
where the time goes in v2:
time: 95.2 us; the launch traced here: 95 us
  Pallas kernels  91.2 us (96%)
  local copies, waits for them, and re-layouts  3.14 us (3%)
    pallas_call x1, Pallas kernels, per_device(): pl.pallas_call(kernel, out_shape=(jax.ShapeDtypeStruct((ROWS, FEAT), BF16...  91.2 us
    unnamed x2, local copies, waits for them, and re-layouts  3.14 us

profile of v2, /device:TPU:1, one launch (start us, length us, event | category | flops | bytes accessed | tf_op | source)
XLA Modules:
  0.0 95.0 jit_solution(286563533542866026)
XLA Ops:
  0.6 91.2 %graph.1 = (bf16[512,128]{1,0:T(8,128)(2,1)}, f32[256,128]{1,0:T(8,128)}) custom-call(bf16[512,128]{1,0:T(8,128)(2,1)} %feat_hbm.1, bf16[512,2048]{1,0:T(8,128)(2,1)} %band_hbm.1, bf16[512,256]{1,0:T(8,128)(2,1)} %far_hbm.1, s32[1,256]{1,0:T(1,128)} %bitcast.1, bf16[128,256]{1,0:T(8,128)(2,1)} %one_hbm.1, bf16[256,128]{1,0:T(8,128)(2,1)} %two_hbm.1, ...), custom_call_target="tpu_custom_call" | custom-call | tf_op jit(solution)/shard_map/graph/pallas_call | solution.py:345
  91.9 1.6 %copy.11 = bf16[512,128]{1,0:T(8,128)(2,1)} copy(bf16[512,128]{1,0:T(8,128)(2,1)} %get-tuple-element.4) | data formatting | bytes 262144
  93.5 1.6 %copy.12 = f32[256,128]{1,0:T(8,128)} copy(f32[256,128]{1,0:T(8,128)} %get-tuple-element.5) | data formatting | bytes 262144

commit v3 on v2

--- a/solution.py
+++ b/solution.py
@@ -116,8 +116,6 @@
     for d in y_order:
         pl.semaphore_signal(y_sem, inc=1, device_id=(y_peer(d), r), device_id_type=MESH)
     pl.semaphore_wait(y_sem, Y - 1)
-    for d in rep_order:
-        pl.semaphore_signal(rep_sem, inc=1, device_id=(i, rep_peer(d)), device_id_type=MESH)
 
     def far_start(layer, low, high):
         @pl.loop(low, high)
@@ -177,6 +175,8 @@
             pltpu.make_async_copy(source, blocks.at[layer, 0], block_recv.at[layer, 0]).start()
 
     hand_first(0, feat.at[own])
+    for d in rep_order:
+        pl.semaphore_signal(rep_sem, inc=1, device_id=(i, rep_peer(d)), device_id_type=MESH)
     far_start(0, 0, N // 2)
     pl.semaphore_wait(rep_sem, R - 1)
     straight(0, feat.at[own])
@@ -261,7 +261,7 @@
 
     grad_in[mine] = grad_cut[mine]
     wait_in(grad_in.at[pl.ds(0, GROUPS - 1)], grad_recv)
-    grad_z[z] = jnp.sum(grad_in[...].astype(F32), axis=0)
+    grad_z[z] = jnp.sum(grad_in[...].astype(F32), axis=0).astype(BF16)
     for d in z_order:
         remote(grad_z.at[z], grad_z.at[z], z_send, z_recv, z_peer(d), r).start()
 
@@ -270,7 +270,7 @@
         remote(score_all.at[own], score_all.at[own], sa_send, sa_recv, i, rep_peer(d)).start()
 
     wait_in(grad_z.at[pl.ds(0, Z - 1)], z_recv)
-    grad_out[mine] = jnp.sum(grad_z[...], axis=0).astype(BF16)
+    grad_out[mine] = jnp.sum(grad_z[...].astype(F32), axis=0).astype(BF16)
 
     def out_go(slot, blk, rep):
         remote(grad_out.at[mine], grad_out.at[mine], out_send, out_recv, blk, rep).start()
@@ -330,7 +330,7 @@
         vmem((R, PIECE, FEAT), BF16),
         vmem((GROUPS, SHARE, FEAT), BF16),
         vmem((GROUPS, SHARE, FEAT), BF16),
-        vmem((Z, SHARE, FEAT), F32),
+        vmem((Z, SHARE, FEAT), BF16),
         vmem((GROUPS, SHARE, FEAT), BF16),
         vmem((R, PIECE, FEAT), BF16),
         vmem((R, PIECE, FEAT), BF16),

time: 95.2 us -> 95 us (level)
  no operation moved by 1% of the time
where the time goes in v3:
time: 95 us; the launch traced here: 94.8 us
  Pallas kernels  91.1 us (96%)
  local copies, waits for them, and re-layouts  3.14 us (3%)
    pallas_call x1, Pallas kernels, per_device(): pl.pallas_call(kernel, out_shape=(jax.ShapeDtypeStruct((ROWS, FEAT), BF16...  91.1 us
    unnamed x2, local copies, waits for them, and re-layouts  3.14 us

profile of v3, /device:TPU:1, one launch (start us, length us, event | category | flops | bytes accessed | tf_op | source)
XLA Modules:
  0.0 94.8 jit_solution(1756863421807283854)
XLA Ops:
  0.6 91.1 %graph.1 = (bf16[512,128]{1,0:T(8,128)(2,1)}, f32[256,128]{1,0:T(8,128)}) custom-call(bf16[512,128]{1,0:T(8,128)(2,1)} %feat_hbm.1, bf16[512,2048]{1,0:T(8,128)(2,1)} %band_hbm.1, bf16[512,256]{1,0:T(8,128)(2,1)} %far_hbm.1, s32[1,256]{1,0:T(1,128)} %bitcast.1, bf16[128,256]{1,0:T(8,128)(2,1)} %one_hbm.1, bf16[256,128]{1,0:T(8,128)(2,1)} %two_hbm.1, ...), custom_call_target="tpu_custom_call" | custom-call | tf_op jit(solution)/shard_map/graph/pallas_call | solution.py:345
  91.7 1.6 %copy.11 = bf16[512,128]{1,0:T(8,128)(2,1)} copy(bf16[512,128]{1,0:T(8,128)(2,1)} %get-tuple-element.4) | data formatting | bytes 262144
  93.3 1.6 %copy.12 = f32[256,128]{1,0:T(8,128)} copy(f32[256,128]{1,0:T(8,128)} %get-tuple-element.5) | data formatting | bytes 262144
